TPU v7x, 256 devices: a whole 4x4x8 slice. The times are simulated.
256 devices in a mesh: rep: 32 (over y, z_lo, core), fsdp: 8 (over x, z_hi).
Axes of the slice: x: 4, y: 4, z: 8 (z_hi: 2, z_lo: 4; z = z_hi * 4 + z_lo), core: 2. Of those that a mesh axis runs over, the one named last changes fastest.
Arguments:
- tokens: bfloat16 [32, 2, 3072, 4096], P('rep', None, 'fsdp'), may hold values from -6 to 6
- token_ids: int32 [32, 2, 3072], P('rep', None, 'fsdp'), may hold values from 0 to 128004, as said below
- out_grad: bfloat16 [32, 2, 3072, 512], P('rep', None, 'fsdp'), may hold values from -6 to 6
- local_weight: bfloat16 [32, 4096, 512], P('rep', 'fsdp'), may hold values from -6 to 6
- adam_first: float32 [32, 4096, 512], P('rep', 'fsdp'), may hold values from -4 to 4
- adam_second: float32 [32, 4096, 512], P('rep', 'fsdp'), may hold values from 0.05 to 2
- anchor: float32 [4096, 512], P('fsdp'), may hold values from -6 to 6
- outer_momentum: float32 [4096, 512], P('fsdp'), may hold values from -4 to 4
- fragment: int32 [1], replicated, may hold values from 0 to 1
Outputs:
- new_local: bfloat16 [32, 4096, 512], P('rep', 'fsdp')
- new_first: float32 [32, 4096, 512], P('rep', 'fsdp')
- new_second: float32 [32, 4096, 512], P('rep', 'fsdp')
- new_anchor: float32 [4096, 512], P('fsdp')
- new_momentum: float32 [4096, 512], P('fsdp')
Inputs may be any that keep to these rules, and one draw needn't show every extreme that they name: `token_ids`: each device's 384 tokens of one inner step form one sequence: regular ids below 128000, then the padding id 128004 to its end; at least a quarter of them are regular and at least the last one is padding.
All inputs are finite; a program needn't handle non-finite values.
Results may differ from a plain program's by a relative error of at most 0.015.
Values may be sent and summed in bfloat16 or wider, within the bound.
No kernel may reach another device: no remote copies, remote signals or barrier semaphores. Data moves between devices by JAX's collectives and lax.ppermute only.
A program may use at most 128 MiB of HBM per device.

v0:
```python
import functools
import math

import jax
import jax.numpy as jnp
from jax import lax
from jax.experimental import pallas as pl
from jax.experimental.pallas import tpu as pltpu
from jax.sharding import PartitionSpec as P

FRAGS = 2
CHUNKS = 2

beta_first = 0.5
beta_second = 0.95
inner_rate = 0.25
decay_rate = 0.1
adam_eps = 1e-08
outer_rate = 0.7
outer_mu = 0.9
mix_keep = 0.5
pad_token = 128004
XS = 4
FIRST_VMEM = 60 * 1024 * 1024
VMEM = 12 * 1024 * 1024


def z_swap(array):
    return lax.ppermute(array, "fsdp", [(i, i ^ 1) for i in range(2 * XS)])


def x_shift(array, offset):
    pairs = [
        (x * 2 + z, ((x + offset) % XS) * 2 + z) for x in range(XS) for z in range(2)
    ]
    return lax.ppermute(array, "fsdp", pairs)


def rep_swap(array, bit):
    return lax.ppermute(array, "rep", [(i, i ^ bit) for i in range(32)])


def after(value, *earlier):
    return lax.optimization_barrier((value, *earlier))[0]


def params():
    return pltpu.CompilerParams(vmem_limit_bytes=VMEM)


def cost():
    return pl.CostEstimate(flops=1000, bytes_accessed=1000, transcendentals=0)


def copy_body(x_at, *refs):
    for source, target in zip(refs[:XS], refs[XS:], strict=True):
        target[...] = source[0, 0]


def arrange(x_at, tokens, step, limit):
    count, width = tokens.shape[2:]
    cut = width // XS
    tile = count // 2

    def taken(offset):
        return lambda i, x: (0, step, i, lax.rem(x[0] + offset, XS))

    return pl.pallas_call(
        copy_body,
        grid_spec=pltpu.PrefetchScalarGridSpec(
            num_scalar_prefetch=1,
            grid=(count // tile,),
            in_specs=[pl.BlockSpec((1, 1, tile, cut), taken(o)) for o in range(XS)],
            out_specs=[pl.BlockSpec((tile, cut), lambda i, x: (i, 0))] * XS,
        ),
        out_shape=[jax.ShapeDtypeStruct((count, cut), tokens.dtype)] * XS,
        compiler_params=pltpu.CompilerParams(vmem_limit_bytes=limit),
        cost_estimate=cost(),
    )(x_at, *[tokens] * XS)


def halves_of(block, z_at):
    rows = block.shape[1] // 2
    mine = block[:, pl.ds(pl.multiple_of(z_at * rows, rows), rows)]
    theirs = block[:, pl.ds(pl.multiple_of((1 - z_at) * rows, rows), rows)]
    return mine, theirs


def forward_body(z_at, *refs):
    blocks, (weight, other), parts = refs[:XS], refs[XS : XS + 2], refs[XS + 2 :]
    for block, part in zip(blocks, parts, strict=True):
        mine, theirs = halves_of(block, z_at[0])
        total = jnp.dot(mine, weight[...], preferred_element_type=jnp.float32)
        total += jnp.dot(theirs, other[...], preferred_element_type=jnp.float32)
        part[...] = total.astype(part.dtype)


def forward(z_at, blocks, weight, other, column, chunk):
    count, cut = blocks[0].shape
    rows = cut // 2
    tile = count // 2
    weights = pl.BlockSpec((rows, chunk), lambda i, z: (0, column))
    return pl.pallas_call(
        forward_body,
        grid_spec=pltpu.PrefetchScalarGridSpec(
            num_scalar_prefetch=1,
            grid=(count // tile,),
            in_specs=[pl.BlockSpec((tile, cut), lambda i, z: (i, 0))] * XS + [weights] * 2,
            out_specs=[pl.BlockSpec((tile, chunk), lambda i, z: (i, 0))] * XS,
        ),
        out_shape=[
            jax.ShapeDtypeStruct((count, chunk), jnp.bfloat16 if o else jnp.float32)
            for o in range(XS)
        ],
        compiler_params=params(),
        cost_estimate=cost(),
    )(z_at, *blocks, weight, other)


def slope_body(scale, *refs):
    parts, grads, back = refs[:XS], refs[XS], refs[XS + 1]
    scores = parts[0][...]
    for part in parts[1:]:
        scores += part[...].astype(jnp.float32)
    scores = scale * scores
    logistic = jax.nn.sigmoid(scores)
    slope = logistic * (1.0 + scores * (1.0 - logistic))
    back[...] = (grads[...].astype(jnp.float32) * slope).astype(back.dtype)


def slope(scale, parts, grads, column):
    count, chunk = parts[0].shape
    tile = count // 2
    own = pl.BlockSpec((tile, chunk), lambda i: (i, 0))
    return pl.pallas_call(
        functools.partial(slope_body, scale),
        grid=(count // tile,),
        in_specs=[own] * XS + [pl.BlockSpec((tile, chunk), lambda i: (i, column))],
        out_specs=own,
        out_shape=jax.ShapeDtypeStruct((count, chunk), jnp.bfloat16),
        compiler_params=params(),
        cost_estimate=cost(),
    )(*parts, grads)


def backward_body(scale, z_at, *refs):
    blocks, backs = refs[:XS], refs[XS : 2 * XS]
    mine, theirs, mine_sum, theirs_sum = refs[2 * XS :]
    at = pl.program_id(0)

    @pl.when(at == 0)
    def _():
        mine_sum[...] = jnp.zeros_like(mine_sum)
        theirs_sum[...] = jnp.zeros_like(theirs_sum)

    for total, half in ((theirs_sum, 1), (mine_sum, 0)):
        more = 0.0
        for block, back in zip(blocks, backs, strict=True):
            more += lax.dot_general(
                halves_of(block, z_at[0])[half],
                back[...],
                (((0,), (0,)), ((), ())),
                preferred_element_type=jnp.float32,
            )
        total[...] += more

    @pl.when(at == pl.num_programs(0) - 1)
    def _():
        mine[...] = scale * mine_sum[...]
        theirs[...] = (scale * theirs_sum[...]).astype(theirs.dtype)


def backward(scale, z_at, blocks, backs):
    count, cut = blocks[0].shape
    chunk = backs[0].shape[1]
    rows = cut // 2
    tile = count // 2
    out = pl.BlockSpec((rows, chunk), lambda i, z: (0, 0))
    return pl.pallas_call(
        functools.partial(backward_body, scale),
        grid_spec=pltpu.PrefetchScalarGridSpec(
            num_scalar_prefetch=1,
            grid=(count // tile,),
            in_specs=[pl.BlockSpec((tile, cut), lambda i, z: (i, 0))] * XS
            + [pl.BlockSpec((tile, chunk), lambda i, z: (i, 0))] * XS,
            out_specs=[out, out],
            scratch_shapes=[pltpu.VMEM((rows, chunk), jnp.float32)] * 2,
        ),
        out_shape=[
            jax.ShapeDtypeStruct((rows, chunk), jnp.float32),
            jax.ShapeDtypeStruct((rows, chunk), jnp.bfloat16),
        ],
        compiler_params=params(),
        cost_estimate=cost(),
    )(z_at, *blocks, *backs)


def adam_values(mine, received, first, second, weight):
    grad = mine[...] + received[...].astype(jnp.float32)
    first = beta_first * first[...] + (1.0 - beta_first) * grad
    second = beta_second * second[...] + (1.0 - beta_second) * grad * grad
    master = weight[...].astype(jnp.float32)
    master = master - inner_rate * (
        first / (jnp.sqrt(second) + adam_eps) + decay_rate * master
    )
    return first, second, master.astype(jnp.bfloat16)


def adam_body(mine, received, first, second, weight, first_out, second_out, weight_out):
    first_out[...], second_out[...], weight_out[...] = adam_values(
        mine, received, first, second, weight
    )


def adam(mine, received, first, second, weight, column):
    rows, chunk = mine.shape
    height = rows // 2
    own = pl.BlockSpec((height, chunk), lambda i: (i, 0))
    whole = pl.BlockSpec((height, chunk), lambda i: (i, column))
    return pl.pallas_call(
        adam_body,
        grid=(rows // height,),
        in_specs=[own, own, whole, whole, whole],
        out_specs=[own, own, own],
        out_shape=[
            jax.ShapeDtypeStruct((rows, chunk), jnp.float32),
            jax.ShapeDtypeStruct((rows, chunk), jnp.float32),
            jax.ShapeDtypeStruct((rows, chunk), jnp.bfloat16),
        ],
        compiler_params=params(),
        cost_estimate=cost(),
    )(mine, received, first, second, weight)


def finish_body(
    column, fragment, mine, received, first, second, weight, anchor, *rest
):
    first_out, second_out, weight_out = rest[-3:]
    first_out[...], second_out[...], trained = adam_values(
        mine, received, first, second, weight
    )
    chunk = trained.shape[1]
    lanes = lax.broadcasted_iota(jnp.int32, trained.shape, 1) + column * chunk
    rostered = lanes // (CHUNKS * chunk // FRAGS) == fragment[0]
    mixed = mix_keep * trained.astype(jnp.float32) + (1.0 - mix_keep) * anchor[...]
    weight_out[...] = jnp.where(rostered, mixed.astype(jnp.bfloat16), trained)


def finish(fragment, mine, received, first, second, weight, anchor, earlier, column):
    rows, chunk = mine.shape
    height = rows // 2
    own = pl.BlockSpec((height, chunk), lambda i, f: (i, 0))
    whole = pl.BlockSpec((height, chunk), lambda i, f: (i, column))
    shape = (rows, chunk * CHUNKS)
    return pl.pallas_call(
        functools.partial(finish_body, column),
        grid_spec=pltpu.PrefetchScalarGridSpec(
            num_scalar_prefetch=1,
            grid=(rows // height,),
            in_specs=[own] * 5 + [whole] + [pl.BlockSpec(memory_space=pl.ANY)] * len(earlier),
            out_specs=[whole] * 3,
        ),
        out_shape=[
            jax.ShapeDtypeStruct(shape, jnp.float32),
            jax.ShapeDtypeStruct(shape, jnp.float32),
            jax.ShapeDtypeStruct(shape, jnp.bfloat16),
        ],
        input_output_aliases={7 + i: i for i in range(len(earlier))},
        compiler_params=params(),
        cost_estimate=cost(),
    )(fragment, mine, received, first, second, weight, anchor, *earlier)


def local(
    tokens,
    token_ids,
    out_grad,
    local_weight,
    adam_first,
    adam_second,
    anchor,
    outer_momentum,
    fragment,
):
    steps, token_count, width = tokens.shape[1:]
    proj_scale = 1.0 / math.sqrt(width)
    columns = local_weight.shape[2]
    piece_width = columns // FRAGS
    chunk = columns // CHUNKS
    fsdp_at = lax.axis_index("fsdp")
    x_at = (fsdp_at // 2).astype(jnp.int32)[None]
    z_at = (fsdp_at % 2).astype(jnp.int32)[None]

    start = local_weight[0]
    total = lax.dynamic_slice_in_dim(start, fragment[0] * piece_width, piece_width, 1)
    rep_bits = [1, 2, 8, 16, 4]

    def add_replicas(total):
        bit = rep_bits.pop(0)
        total = total.astype(jnp.float32) + rep_swap(total, bit).astype(jnp.float32)
        return total.astype(jnp.bfloat16) if rep_bits else total

    other = z_swap(start)
    cuts = [arrange(x_at, tokens, s, VMEM if s else FIRST_VMEM) for s in range(steps)]
    masked = [
        jnp.where((token_ids[0, s] != pad_token)[:, None], out_grad[0, s], 0)
        for s in range(steps)
    ]

    def spread(pieces):
        return [pieces[0]] + [x_shift(pieces[o], o) for o in range(1, XS)]

    state = [(adam_first[0], adam_second[0], start, other, c) for c in range(CHUNKS)]
    for _ in range(len(rep_bits)):
        total = add_replicas(total)
    average = jnp.tile(total / lax.axis_size("rep"), (1, FRAGS))
    rostered = lax.broadcasted_iota(jnp.int32, (1, columns), 1) // piece_width == fragment[0]
    pseudo = anchor - average
    moment_new = outer_mu * outer_momentum + pseudo
    anchor_new = anchor - outer_rate * (pseudo + outer_mu * moment_new)
    new_anchor = jnp.where(rostered, anchor_new, anchor)
    new_momentum = jnp.where(rostered, moment_new, outer_momentum)
    blocks = spread(cuts[0])
    last = after(cuts[1][0], *masked)
    finished = ()
    for step in range(steps):
        parts, backs, grads = {}, {}, {}
        for c in range(CHUNKS):
            first, second, weight, other, column = state[c]
            parts[c] = forward(z_at, blocks, after(weight, last), other, column, chunk)
            last = parts[c][0]
        for c in range(CHUNKS):
            gathered = [parts[c][0]] + [x_shift(parts[c][o], -o) for o in range(1, XS)]
            gathered[0] = after(gathered[0], last)
            last = slope(proj_scale, gathered, masked[step], c)
            backs[c] = last
        for c in range(CHUNKS):
            spread_backs = [after(backs[c], last)] + [x_shift(backs[c], o) for o in range(1, XS)]
            grads[c] = backward(proj_scale, z_at, blocks, spread_backs)
            last = grads[c][0]
        if step + 1 < steps:
            blocks_next = spread([after(cut, *spread_backs) for cut in cuts[step + 1]])
        for c in range(CHUNKS):
            first, second, weight, other, column = state[c]
            mine, theirs = grads[c]
            received = z_swap(theirs)
            mine = after(mine, last)
            if step + 1 < steps:
                first, second, weight = adam(mine, received, first, second, weight, column)
                last = first
                state[c] = (first, second, weight, z_swap(weight), 0)
            else:
                finished = finish(
                    fragment, mine, received, first, second, weight, new_anchor, finished, c
                )
                last = finished[0]
        if step + 1 < steps:
            blocks = blocks_next
    new_first, new_second, new_local = finished
    return (new_local[None], new_first[None], new_second[None], new_anchor, new_momentum)


def solution(mesh):
    return jax.shard_map(
        local,
        mesh=mesh,
        in_specs=(
            P("rep", None, "fsdp", None),
            P("rep", None, "fsdp"),
            P("rep", None, "fsdp", None),
            P("rep", "fsdp", None),
            P("rep", "fsdp", None),
            P("rep", "fsdp", None),
            P("fsdp", None),
            P("fsdp", None),
            P(),
        ),
        out_specs=(
            P("rep", "fsdp", None),
            P("rep", "fsdp", None),
            P("rep", "fsdp", None),
            P("fsdp", None),
            P("fsdp", None),
        ),
        check_vma=False,
    )
```

profile of v0, /device:TPU:1, one launch (start us, length us, event | category | flops | bytes accessed | tf_op | source)
XLA Modules:
  0.0 191.4 jit_solution(11269610874538224823)
XLA Ops:
  0.7 3.2 %shard_map.129 = (bf16[384,1024]{1,0:T(8,128)(2,1)}, bf16[384,1024]{1,0:T(8,128)(2,1)}, bf16[384,1024]{1,0:T(8,128)(2,1)}, bf16[384,1024]{1,0:T(8,128)(2,1)}) custom-call(s32[1]{0:T(128)} %bitcast.1.x_at, bf16[1,2,384,4096]{3,2,1,0:T(8,128)(2,1)} %refs_3_.3, bf16[1,2,384,4096]{3,2,1,0:T(8,128)(2,1)} %refs_3_.3, bf16[1,2,384,4096]{3,2,1,0:T(8,128)(2,1)} %refs_3_.3, ...), custom_call_target="tpu_custom_call" | custom-call | flops 1000 | bytes 1000 | tf_op jit(solution)/shard_map/pallas_call | solution.py:68
  3.9 2.0 %collective-permute-start = (bf16[384,1024]{1,0:T(8,128)(2,1)}, bf16[384,1024]{1,0:T(8,128)(2,1)S(1)}, u32[]{:S(2)}, u32[]{:S(2)}) collective-permute-start(bf16[384,1024]{1,0:T(8,128)(2,1)} %get-tuple-element.70), channel_id=1, source_target_pairs={{0,2},{1,3},{2,4},{3,5},{4,6},{5,7},{6,0},{7,1},{8,10},{9,11},{10,... | collective-permute-start | bytes 2359304 | tf_op jit(solution)/shard_map/ppermute | solution.py:36
  5.9 2.5 %collective-permute-start.1 = (bf16[384,1024]{1,0:T(8,128)(2,1)}, bf16[384,1024]{1,0:T(8,128)(2,1)S(1)}, u32[]{:S(2)}, u32[]{:S(2)}) collective-permute-start(bf16[384,1024]{1,0:T(8,128)(2,1)} %get-tuple-element.71), channel_id=1, source_target_pairs={{0,4},{1,5},{2,6},{3,7},{4,0},{5,1},{6,2},{7,3},{8,12},{9,13},{10,... | collective-permute-start | bytes 2359304 | tf_op jit(solution)/shard_map/ppermute | solution.py:36
  9.5 6.9 %collective-permute-start.3 = (bf16[512,512]{1,0:T(8,128)(2,1)S(1)}, bf16[512,512]{1,0:T(8,128)(2,1)S(1)}, u32[]{:S(2)}, u32[]{:S(2)}) collective-permute-start(bf16[512,512]{1,0:T(8,128)(2,1)S(1)} %bitcast.23), channel_id=1, source_target_pairs={{0,1},{1,0},{2,3},{3,2},{4,5},{5,4},{6,7},{7,6},{8,9},{9,8},{10,11... | collective-permute-start | bytes 1572872 | tf_op jit(solution)/shard_map/ppermute | solution.py:29
  17.8 1.8 collective-permute-start.36
  19.6 9.6 %collective-permute-done.3.refs_5_ = bf16[512,512]{1,0:T(8,128)(2,1)S(1)} collective-permute-done((bf16[512,512]{1,0:T(8,128)(2,1)S(1)}, bf16[512,512]{1,0:T(8,128)(2,1)S(1)}, u32[]{:S(2)}, u32[]{:S(2)}) %collective-permute-start.3) | collective-permute-done | bytes 524320 | tf_op jit(solution)/shard_map/ppermute | solution.py:29
  29.2 13.1 %collective-permute-done.1.refs_2_ = bf16[384,1024]{1,0:T(8,128)(2,1)S(1)} collective-permute-done((bf16[384,1024]{1,0:T(8,128)(2,1)}, bf16[384,1024]{1,0:T(8,128)(2,1)S(1)}, u32[]{:S(2)}, u32[]{:S(2)}) %collective-permute-start.1) | collective-permute-done | bytes 786464 | tf_op jit(solution)/shard_map/ppermute | solution.py:36
  44.8 3.0 %collective-permute-start.4 = (bf16[384,256]{1,0:T(8,128)(2,1)S(1)}, bf16[384,256]{1,0:T(8,128)(2,1)S(1)}, u32[]{:S(2)}, u32[]{:S(2)}) collective-permute-start(bf16[384,256]{1,0:T(8,128)(2,1)S(1)} %get-tuple-element.77), channel_id=1, source_target_pairs={{0,6},{1,7},{2,0},{3,1},{4,2},{5,3},{6,4},{7,5},{8,14},{9,15},{10,... | collective-permute-start | bytes 589832 | tf_op jit(solution)/shard_map/ppermute | solution.py:36
  51.1 2.1 %collective-permute-start.7 = (bf16[384,256]{1,0:T(8,128)(2,1)S(1)}, bf16[384,256]{1,0:T(8,128)(2,1)S(1)}, u32[]{:S(2)}, u32[]{:S(2)}) collective-permute-start(bf16[384,256]{1,0:T(8,128)(2,1)S(1)} %get-tuple-element.81), channel_id=1, source_target_pairs={{0,6},{1,7},{2,0},{3,1},{4,2},{5,3},{6,4},{7,5},{8,14},{9,15},{10,... | collective-permute-start | bytes 589832 | tf_op jit(solution)/shard_map/ppermute | solution.py:36
  53.1 1.9 collective-permute-done.4.refs_1_
  55.1 4.5 %collective-permute-start.9 = (bf16[384,256]{1,0:T(8,128)(2,1)S(1)}, bf16[384,256]{1,0:T(8,128)(2,1)S(1)}, u32[]{:S(2)}, u32[]{:S(2)}) collective-permute-start(bf16[384,256]{1,0:T(8,128)(2,1)S(1)} %get-tuple-element.83), channel_id=1, source_target_pairs={{0,2},{1,3},{2,4},{3,5},{4,6},{5,7},{6,0},{7,1},{8,10},{9,11},{10,... | collective-permute-start | bytes 589832 | tf_op jit(solution)/shard_map/ppermute | solution.py:36
  62.2 1.9 %collective-permute-start.37 = (bf16[512,256]{1,0:T(8,128)(2,1)S(1)}, bf16[512,256]{1,0:T(8,128)(2,1)S(1)}, u32[]{:S(2)}, u32[]{:S(2)}) collective-permute-start(bf16[512,256]{1,0:T(8,128)(2,1)S(1)} %add_convert_fusion.3), channel_id=1, source_target_pairs={{0,16},{8,24},{16,0},{24,8},{32,48},{40,56},{48,32},{56,40},{64,80... | collective-permute-start | bytes 786440 | tf_op jit(solution)/shard_map/ppermute | solution.py:40
  64.2 3.3 %collective-permute-start.12 = (bf16[384,256]{1,0:T(8,128)(2,1)S(1)}, bf16[384,256]{1,0:T(8,128)(2,1)S(1)}, u32[]{:S(2)}, u32[]{:S(2)}) collective-permute-start(bf16[384,256]{1,0:T(8,128)(2,1)S(1)} %shard_map.132.refs_4_), channel_id=1, source_target_pairs={{0,6},{1,7},{2,0},{3,1},{4,2},{5,3},{6,4},{7,5},{8,14},{9,15},{10,... | collective-permute-start | bytes 589832 | tf_op jit(solution)/shard_map/ppermute | solution.py:36
  68.6 4.7 %collective-permute-done.10.refs_5_ = bf16[384,256]{1,0:T(8,128)(2,1)S(1)} collective-permute-done((bf16[384,256]{1,0:T(8,128)(2,1)S(1)}, bf16[384,256]{1,0:T(8,128)(2,1)S(1)}, u32[]{:S(2)}, u32[]{:S(2)}) %collective-permute-start.10) | collective-permute-done | bytes 196640 | tf_op jit(solution)/shard_map/ppermute | solution.py:36
  73.6 1.8 collective-permute-done.11.refs_6_
  77.8 7.1 %collective-permute-start.19 = (bf16[512,256]{1,0:T(8,128)(2,1)S(1)}, bf16[512,256]{1,0:T(8,128)(2,1)S(1)}, u32[]{:S(2)}, u32[]{:S(2)}) collective-permute-start(bf16[512,256]{1,0:T(8,128)(2,1)S(1)} %get-tuple-element.96), channel_id=1, source_target_pairs={{0,1},{1,0},{2,3},{3,2},{4,5},{5,4},{6,7},{7,6},{8,9},{9,8},{10,11... | collective-permute-start | bytes 786440 | tf_op jit(solution)/shard_map/ppermute | solution.py:29
  91.4 5.2 %collective-permute-start.20 = (bf16[512,256]{1,0:T(8,128)(2,1)S(1)}, bf16[512,256]{1,0:T(8,128)(2,1)S(1)}, u32[]{:S(2)}, u32[]{:S(2)}) collective-permute-start(bf16[512,256]{1,0:T(8,128)(2,1)S(1)} %get-tuple-element.99), channel_id=1, source_target_pairs={{0,1},{1,0},{2,3},{3,2},{4,5},{5,4},{6,7},{7,6},{8,9},{9,8},{10,11... | collective-permute-start | bytes 786440 | tf_op jit(solution)/shard_map/ppermute | solution.py:29
  97.2 1.8 collective-permute-start.21
  99.1 4.2 %collective-permute-done.20.received = bf16[512,256]{1,0:T(8,128)(2,1)S(1)} collective-permute-done((bf16[512,256]{1,0:T(8,128)(2,1)S(1)}, bf16[512,256]{1,0:T(8,128)(2,1)S(1)}, u32[]{:S(2)}, u32[]{:S(2)}) %collective-permute-start.20) | collective-permute-done | bytes 262176 | tf_op jit(solution)/shard_map/ppermute | solution.py:29
  103.2 2.4 %collective-permute-start.39 = (bf16[512,256]{1,0:T(8,128)(2,1)S(1)}, bf16[512,256]{1,0:T(8,128)(2,1)S(1)}, u32[]{:S(2)}, u32[]{:S(2)}) collective-permute-start(bf16[512,256]{1,0:T(8,128)(2,1)S(1)} %add_convert_fusion.1), channel_id=1, source_target_pairs={{0,128},{8,136},{16,144},{24,152},{32,160},{40,168},{48,176},{56,1... | collective-permute-start | bytes 786440 | tf_op jit(solution)/shard_map/ppermute | solution.py:40
  106.3 6.5 %collective-permute-done.21.refs_5_ = bf16[512,256]{1,0:T(8,128)(2,1)S(1)} collective-permute-done((bf16[512,256]{1,0:T(8,128)(2,1)S(1)}, bf16[512,256]{1,0:T(8,128)(2,1)S(1)}, u32[]{:S(2)}, u32[]{:S(2)}) %collective-permute-start.21) | collective-permute-done | bytes 262176 | tf_op jit(solution)/shard_map/ppermute | solution.py:29
  112.7 6.1 %collective-permute-start.22 = (bf16[512,256]{1,0:T(8,128)(2,1)S(1)}, bf16[512,256]{1,0:T(8,128)(2,1)S(1)}, u32[]{:S(2)}, u32[]{:S(2)}) collective-permute-start(bf16[512,256]{1,0:T(8,128)(2,1)S(1)} %get-tuple-element.105.refs_4_.weight), channel_id=1, source_target_pairs={{0,1},{1,0},{2,3},{3,2},{4,5},{5,4},{6,7},{7,6},{8,9},{9,8},{10,11... | collective-permute-start | bytes 786440 | tf_op jit(solution)/shard_map/ppermute | solution.py:29
  118.9 5.5 %collective-permute-done.16.refs_1_ = bf16[384,1024]{1,0:T(8,128)(2,1)S(1)} collective-permute-done((bf16[384,1024]{1,0:T(8,128)(2,1)S(1)}, bf16[384,1024]{1,0:T(8,128)(2,1)S(1)}, u32[]{:S(2)}, u32[]{:S(2)}) %collective-permute-start.16) | collective-permute-done | bytes 786464 | tf_op jit(solution)/shard_map/ppermute | solution.py:36
  125.6 3.3 %collective-permute-start.23 = (bf16[384,256]{1,0:T(8,128)(2,1)S(1)}, bf16[384,256]{1,0:T(8,128)(2,1)S(1)}, u32[]{:S(2)}, u32[]{:S(2)}) collective-permute-start(bf16[384,256]{1,0:T(8,128)(2,1)S(1)} %get-tuple-element.108), channel_id=1, source_target_pairs={{0,6},{1,7},{2,0},{3,1},{4,2},{5,3},{6,4},{7,5},{8,14},{9,15},{10,... | collective-permute-start | bytes 589832 | tf_op jit(solution)/shard_map/ppermute | solution.py:36
  129.7 8.0 %collective-permute-start.40 = (bf16[512,256]{1,0:T(8,128)(2,1)S(1)}, bf16[512,256]{1,0:T(8,128)(2,1)S(1)}, u32[]{:S(2)}, u32[]{:S(2)}) collective-permute-start(bf16[512,256]{1,0:T(8,128)(2,1)S(1)} %add_convert_fusion), channel_id=1, source_target_pairs={{0,32},{8,40},{16,48},{24,56},{32,0},{40,8},{48,16},{56,24},{64,96... | collective-permute-start | bytes 786440 | tf_op jit(solution)/shard_map/ppermute | solution.py:40
  139.0 2.0 %collective-permute-start.26 = (bf16[384,256]{1,0:T(8,128)(2,1)S(1)}, bf16[384,256]{1,0:T(8,128)(2,1)S(1)}, u32[]{:S(2)}, u32[]{:S(2)}) collective-permute-start(bf16[384,256]{1,0:T(8,128)(2,1)S(1)} %get-tuple-element.112), channel_id=1, source_target_pairs={{0,6},{1,7},{2,0},{3,1},{4,2},{5,3},{6,4},{7,5},{8,14},{9,15},{10,... | collective-permute-start | bytes 589832 | tf_op jit(solution)/shard_map/ppermute | solution.py:36
  142.0 2.0 %collective-permute-start.29 = (bf16[384,256]{1,0:T(8,128)(2,1)S(1)}, bf16[384,256]{1,0:T(8,128)(2,1)S(1)}, u32[]{:S(2)}, u32[]{:S(2)}) collective-permute-start(bf16[384,256]{1,0:T(8,128)(2,1)S(1)} %shard_map.140.refs_4_), channel_id=1, source_target_pairs={{0,2},{1,3},{2,4},{3,5},{4,6},{5,7},{6,0},{7,1},{8,10},{9,11},{10,... | collective-permute-start | bytes 589832 | tf_op jit(solution)/shard_map/ppermute | solution.py:36
  147.1 2.8 %collective-permute-start.31 = (bf16[384,256]{1,0:T(8,128)(2,1)S(1)}, bf16[384,256]{1,0:T(8,128)(2,1)S(1)}, u32[]{:S(2)}, u32[]{:S(2)}) collective-permute-start(bf16[384,256]{1,0:T(8,128)(2,1)S(1)} %shard_map.140.refs_4_), channel_id=1, source_target_pairs={{0,6},{1,7},{2,0},{3,1},{4,2},{5,3},{6,4},{7,5},{8,14},{9,15},{10,... | collective-permute-start | bytes 589832 | tf_op jit(solution)/shard_map/ppermute | solution.py:36
  149.9 3.2 %collective-permute-done.28.refs_3_ = bf16[384,256]{1,0:T(8,128)(2,1)S(1)} collective-permute-done((bf16[384,256]{1,0:T(8,128)(2,1)S(1)}, bf16[384,256]{1,0:T(8,128)(2,1)S(1)}, u32[]{:S(2)}, u32[]{:S(2)}) %collective-permute-start.28) | collective-permute-done | bytes 196640 | tf_op jit(solution)/shard_map/ppermute | solution.py:36
  153.8 5.3 %collective-permute-done.29.refs_5_ = bf16[384,256]{1,0:T(8,128)(2,1)S(1)} collective-permute-done((bf16[384,256]{1,0:T(8,128)(2,1)S(1)}, bf16[384,256]{1,0:T(8,128)(2,1)S(1)}, u32[]{:S(2)}, u32[]{:S(2)}) %collective-permute-start.29) | collective-permute-done | bytes 196640 | tf_op jit(solution)/shard_map/ppermute | solution.py:36
  161.5 4.9 %collective-permute-done.32.refs_5_ = bf16[384,256]{1,0:T(8,128)(2,1)S(1)} collective-permute-done((bf16[384,256]{1,0:T(8,128)(2,1)S(1)}, bf16[384,256]{1,0:T(8,128)(2,1)S(1)}, u32[]{:S(2)}, u32[]{:S(2)}) %collective-permute-start.32) | collective-permute-done | bytes 196640 | tf_op jit(solution)/shard_map/ppermute | solution.py:36
  172.5 17.5 %collective-permute-done.41.received = bf16[512,256]{1,0:T(8,128)(2,1)S(1)} collective-permute-done((bf16[512,256]{1,0:T(8,128)(2,1)S(1)}, bf16[512,256]{1,0:T(8,128)(2,1)S(1)}, u32[]{:S(2)}, u32[]{:S(2)}) %collective-permute-start.41) | collective-permute-done | bytes 262176 | tf_op jit(solution)/shard_map/ppermute | solution.py:29
  (105 shorter events, 39.5 us)
Async XLA Ops:
  3.9 25.4 %collective-permute-start = (bf16[384,1024]{1,0:T(8,128)(2,1)}, bf16[384,1024]{1,0:T(8,128)(2,1)S(1)}, u32[]{:S(2)}, u32[]{:S(2)}) collective-permute-start(bf16[384,1024]{1,0:T(8,128)(2,1)} %get-tuple-element.70), channel_id=1, source_target_pairs={{0,2},{1,3},{2,4},{3,5},{4,6},{5,7},{6,0},{7,1},{8,10},{9,11},{10,... | collective-permute-start | bytes 2359304 | tf_op jit(solution)/shard_map/ppermute | solution.py:36
  5.9 36.5 %collective-permute-start.1 = (bf16[384,1024]{1,0:T(8,128)(2,1)}, bf16[384,1024]{1,0:T(8,128)(2,1)S(1)}, u32[]{:S(2)}, u32[]{:S(2)}) collective-permute-start(bf16[384,1024]{1,0:T(8,128)(2,1)} %get-tuple-element.71), channel_id=1, source_target_pairs={{0,4},{1,5},{2,6},{3,7},{4,0},{5,1},{6,2},{7,3},{8,12},{9,13},{10,... | collective-permute-start | bytes 2359304 | tf_op jit(solution)/shard_map/ppermute | solution.py:36
  8.4 34.0 %collective-permute-start.2 = (bf16[384,1024]{1,0:T(8,128)(2,1)}, bf16[384,1024]{1,0:T(8,128)(2,1)S(1)}, u32[]{:S(2)}, u32[]{:S(2)}) collective-permute-start(bf16[384,1024]{1,0:T(8,128)(2,1)} %get-tuple-element.72), channel_id=1, source_target_pairs={{0,6},{1,7},{2,0},{3,1},{4,2},{5,3},{6,4},{7,5},{8,14},{9,15},{10,... | collective-permute-start | bytes 2359304 | tf_op jit(solution)/shard_map/ppermute | solution.py:36
  9.5 19.7 %collective-permute-start.3 = (bf16[512,512]{1,0:T(8,128)(2,1)S(1)}, bf16[512,512]{1,0:T(8,128)(2,1)S(1)}, u32[]{:S(2)}, u32[]{:S(2)}) collective-permute-start(bf16[512,512]{1,0:T(8,128)(2,1)S(1)} %bitcast.23), channel_id=1, source_target_pairs={{0,1},{1,0},{2,3},{3,2},{4,5},{5,4},{6,7},{7,6},{8,9},{9,8},{10,11... | collective-permute-start | bytes 1572872 | tf_op jit(solution)/shard_map/ppermute | solution.py:29
  17.8 42.6 %collective-permute-start.36 = (bf16[512,256]{1,0:T(8,128)(2,1)}, bf16[512,256]{1,0:T(8,128)(2,1)}, u32[]{:S(2)}, u32[]{:S(2)}) collective-permute-start(bf16[512,256]{1,0:T(8,128)(2,1)} %dynamic-slice_bitcast_fusion), channel_id=1, source_target_pairs={{0,8},{8,0},{16,24},{24,16},{32,40},{40,32},{48,56},{56,48},{64,72... | collective-permute-start | bytes 786440 | tf_op jit(solution)/shard_map/ppermute | solution.py:40
  47.8 12.3 %collective-permute-start.6 = (bf16[384,256]{1,0:T(8,128)(2,1)S(1)}, bf16[384,256]{1,0:T(8,128)(2,1)S(1)}, u32[]{:S(2)}, u32[]{:S(2)}) collective-permute-start(bf16[384,256]{1,0:T(8,128)(2,1)S(1)} %get-tuple-element.79), channel_id=1, source_target_pairs={{0,2},{1,3},{2,4},{3,5},{4,6},{5,7},{6,0},{7,1},{8,10},{9,11},{10,... | collective-permute-start | bytes 589832 | tf_op jit(solution)/shard_map/ppermute | solution.py:36
  55.1 13.0 %collective-permute-start.9 = (bf16[384,256]{1,0:T(8,128)(2,1)S(1)}, bf16[384,256]{1,0:T(8,128)(2,1)S(1)}, u32[]{:S(2)}, u32[]{:S(2)}) collective-permute-start(bf16[384,256]{1,0:T(8,128)(2,1)S(1)} %get-tuple-element.83), channel_id=1, source_target_pairs={{0,2},{1,3},{2,4},{3,5},{4,6},{5,7},{6,0},{7,1},{8,10},{9,11},{10,... | collective-permute-start | bytes 589832 | tf_op jit(solution)/shard_map/ppermute | solution.py:36
  60.3 13.0 %collective-permute-start.10 = (bf16[384,256]{1,0:T(8,128)(2,1)S(1)}, bf16[384,256]{1,0:T(8,128)(2,1)S(1)}, u32[]{:S(2)}, u32[]{:S(2)}) collective-permute-start(bf16[384,256]{1,0:T(8,128)(2,1)S(1)} %shard_map.132.refs_4_), channel_id=1, source_target_pairs={{0,2},{1,3},{2,4},{3,5},{4,6},{5,7},{6,0},{7,1},{8,10},{9,11},{10,... | collective-permute-start | bytes 589832 | tf_op jit(solution)/shard_map/ppermute | solution.py:36
  60.4 15.0 %collective-permute-start.11 = (bf16[384,256]{1,0:T(8,128)(2,1)S(1)}, bf16[384,256]{1,0:T(8,128)(2,1)S(1)}, u32[]{:S(2)}, u32[]{:S(2)}) collective-permute-start(bf16[384,256]{1,0:T(8,128)(2,1)S(1)} %shard_map.132.refs_4_), channel_id=1, source_target_pairs={{0,4},{1,5},{2,6},{3,7},{4,0},{5,1},{6,2},{7,3},{8,12},{9,13},{10,... | collective-permute-start | bytes 589832 | tf_op jit(solution)/shard_map/ppermute | solution.py:36
  62.2 26.0 %collective-permute-start.37 = (bf16[512,256]{1,0:T(8,128)(2,1)S(1)}, bf16[512,256]{1,0:T(8,128)(2,1)S(1)}, u32[]{:S(2)}, u32[]{:S(2)}) collective-permute-start(bf16[512,256]{1,0:T(8,128)(2,1)S(1)} %add_convert_fusion.3), channel_id=1, source_target_pairs={{0,16},{8,24},{16,0},{24,8},{32,48},{40,56},{48,32},{56,40},{64,80... | collective-permute-start | bytes 786440 | tf_op jit(solution)/shard_map/ppermute | solution.py:40
  64.2 11.9 %collective-permute-start.12 = (bf16[384,256]{1,0:T(8,128)(2,1)S(1)}, bf16[384,256]{1,0:T(8,128)(2,1)S(1)}, u32[]{:S(2)}, u32[]{:S(2)}) collective-permute-start(bf16[384,256]{1,0:T(8,128)(2,1)S(1)} %shard_map.132.refs_4_), channel_id=1, source_target_pairs={{0,6},{1,7},{2,0},{3,1},{4,2},{5,3},{6,4},{7,5},{8,14},{9,15},{10,... | collective-permute-start | bytes 589832 | tf_op jit(solution)/shard_map/ppermute | solution.py:36
  68.4 16.6 %collective-permute-start.13 = (bf16[384,256]{1,0:T(8,128)(2,1)S(1)}, bf16[384,256]{1,0:T(8,128)(2,1)S(1)}, u32[]{:S(2)}, u32[]{:S(2)}) collective-permute-start(bf16[384,256]{1,0:T(8,128)(2,1)S(1)} %shard_map.133.refs_4_), channel_id=1, source_target_pairs={{0,2},{1,3},{2,4},{3,5},{4,6},{5,7},{6,0},{7,1},{8,10},{9,11},{10,... | collective-permute-start | bytes 589832 | tf_op jit(solution)/shard_map/ppermute | solution.py:36
  73.3 11.6 %collective-permute-start.14 = (bf16[384,256]{1,0:T(8,128)(2,1)S(1)}, bf16[384,256]{1,0:T(8,128)(2,1)S(1)}, u32[]{:S(2)}, u32[]{:S(2)}) collective-permute-start(bf16[384,256]{1,0:T(8,128)(2,1)S(1)} %shard_map.133.refs_4_), channel_id=1, source_target_pairs={{0,4},{1,5},{2,6},{3,7},{4,0},{5,1},{6,2},{7,3},{8,12},{9,13},{10,... | collective-permute-start | bytes 589832 | tf_op jit(solution)/shard_map/ppermute | solution.py:36
  77.8 13.6 %collective-permute-start.19 = (bf16[512,256]{1,0:T(8,128)(2,1)S(1)}, bf16[512,256]{1,0:T(8,128)(2,1)S(1)}, u32[]{:S(2)}, u32[]{:S(2)}) collective-permute-start(bf16[512,256]{1,0:T(8,128)(2,1)S(1)} %get-tuple-element.96), channel_id=1, source_target_pairs={{0,1},{1,0},{2,3},{3,2},{4,5},{5,4},{6,7},{7,6},{8,9},{9,8},{10,11... | collective-permute-start | bytes 786440 | tf_op jit(solution)/shard_map/ppermute | solution.py:29
  84.9 33.9 %collective-permute-start.18 = (bf16[384,1024]{1,0:T(8,128)(2,1)S(1)}, bf16[384,1024]{1,0:T(8,128)(2,1)S(1)}, u32[]{:S(2)}, u32[]{:S(2)}) collective-permute-start(bf16[384,1024]{1,0:T(8,128)(2,1)S(1)} %get-tuple-element.93), channel_id=1, source_target_pairs={{0,6},{1,7},{2,0},{3,1},{4,2},{5,3},{6,4},{7,5},{8,14},{9,15},{10,... | collective-permute-start | bytes 2359304 | tf_op jit(solution)/shard_map/ppermute | solution.py:36
  86.6 32.3 %collective-permute-start.17 = (bf16[384,1024]{1,0:T(8,128)(2,1)S(1)}, bf16[384,1024]{1,0:T(8,128)(2,1)S(1)}, u32[]{:S(2)}, u32[]{:S(2)}) collective-permute-start(bf16[384,1024]{1,0:T(8,128)(2,1)S(1)} %get-tuple-element.91), channel_id=1, source_target_pairs={{0,4},{1,5},{2,6},{3,7},{4,0},{5,1},{6,2},{7,3},{8,12},{9,13},{10,... | collective-permute-start | bytes 2359304 | tf_op jit(solution)/shard_map/ppermute | solution.py:36
  88.2 36.2 %collective-permute-start.16 = (bf16[384,1024]{1,0:T(8,128)(2,1)S(1)}, bf16[384,1024]{1,0:T(8,128)(2,1)S(1)}, u32[]{:S(2)}, u32[]{:S(2)}) collective-permute-start(bf16[384,1024]{1,0:T(8,128)(2,1)S(1)} %get-tuple-element.89), channel_id=1, source_target_pairs={{0,2},{1,3},{2,4},{3,5},{4,6},{5,7},{6,0},{7,1},{8,10},{9,11},{10,... | collective-permute-start | bytes 2359304 | tf_op jit(solution)/shard_map/ppermute | solution.py:36
  91.4 11.8 %collective-permute-start.20 = (bf16[512,256]{1,0:T(8,128)(2,1)S(1)}, bf16[512,256]{1,0:T(8,128)(2,1)S(1)}, u32[]{:S(2)}, u32[]{:S(2)}) collective-permute-start(bf16[512,256]{1,0:T(8,128)(2,1)S(1)} %get-tuple-element.99), channel_id=1, source_target_pairs={{0,1},{1,0},{2,3},{3,2},{4,5},{5,4},{6,7},{7,6},{8,9},{9,8},{10,11... | collective-permute-start | bytes 786440 | tf_op jit(solution)/shard_map/ppermute | solution.py:29
  97.2 15.5 %collective-permute-start.21 = (bf16[512,256]{1,0:T(8,128)(2,1)S(1)}, bf16[512,256]{1,0:T(8,128)(2,1)S(1)}, u32[]{:S(2)}, u32[]{:S(2)}) collective-permute-start(bf16[512,256]{1,0:T(8,128)(2,1)S(1)} %get-tuple-element.103.refs_4_.weight), channel_id=1, source_target_pairs={{0,1},{1,0},{2,3},{3,2},{4,5},{5,4},{6,7},{7,6},{8,9},{9,8},{10,11... | collective-permute-start | bytes 786440 | tf_op jit(solution)/shard_map/ppermute | solution.py:29
  103.2 26.4 %collective-permute-start.39 = (bf16[512,256]{1,0:T(8,128)(2,1)S(1)}, bf16[512,256]{1,0:T(8,128)(2,1)S(1)}, u32[]{:S(2)}, u32[]{:S(2)}) collective-permute-start(bf16[512,256]{1,0:T(8,128)(2,1)S(1)} %add_convert_fusion.1), channel_id=1, source_target_pairs={{0,128},{8,136},{16,144},{24,152},{32,160},{40,168},{48,176},{56,1... | collective-permute-start | bytes 786440 | tf_op jit(solution)/shard_map/ppermute | solution.py:40
  112.7 25.0 %collective-permute-start.22 = (bf16[512,256]{1,0:T(8,128)(2,1)S(1)}, bf16[512,256]{1,0:T(8,128)(2,1)S(1)}, u32[]{:S(2)}, u32[]{:S(2)}) collective-permute-start(bf16[512,256]{1,0:T(8,128)(2,1)S(1)} %get-tuple-element.105.refs_4_.weight), channel_id=1, source_target_pairs={{0,1},{1,0},{2,3},{3,2},{4,5},{5,4},{6,7},{7,6},{8,9},{9,8},{10,11... | collective-permute-start | bytes 786440 | tf_op jit(solution)/shard_map/ppermute | solution.py:29
  125.6 15.4 %collective-permute-start.23 = (bf16[384,256]{1,0:T(8,128)(2,1)S(1)}, bf16[384,256]{1,0:T(8,128)(2,1)S(1)}, u32[]{:S(2)}, u32[]{:S(2)}) collective-permute-start(bf16[384,256]{1,0:T(8,128)(2,1)S(1)} %get-tuple-element.108), channel_id=1, source_target_pairs={{0,6},{1,7},{2,0},{3,1},{4,2},{5,3},{6,4},{7,5},{8,14},{9,15},{10,... | collective-permute-start | bytes 589832 | tf_op jit(solution)/shard_map/ppermute | solution.py:36
  129.0 12.0 %collective-permute-start.24 = (bf16[384,256]{1,0:T(8,128)(2,1)S(1)}, bf16[384,256]{1,0:T(8,128)(2,1)S(1)}, u32[]{:S(2)}, u32[]{:S(2)}) collective-permute-start(bf16[384,256]{1,0:T(8,128)(2,1)S(1)} %get-tuple-element.109), channel_id=1, source_target_pairs={{0,4},{1,5},{2,6},{3,7},{4,0},{5,1},{6,2},{7,3},{8,12},{9,13},{10,... | collective-permute-start | bytes 589832 | tf_op jit(solution)/shard_map/ppermute | solution.py:36
  129.0 12.7 %collective-permute-start.25 = (bf16[384,256]{1,0:T(8,128)(2,1)S(1)}, bf16[384,256]{1,0:T(8,128)(2,1)S(1)}, u32[]{:S(2)}, u32[]{:S(2)}) collective-permute-start(bf16[384,256]{1,0:T(8,128)(2,1)S(1)} %get-tuple-element.110), channel_id=1, source_target_pairs={{0,2},{1,3},{2,4},{3,5},{4,6},{5,7},{6,0},{7,1},{8,10},{9,11},{10,... | collective-permute-start | bytes 589832 | tf_op jit(solution)/shard_map/ppermute | solution.py:36
  129.7 23.8 %collective-permute-start.40 = (bf16[512,256]{1,0:T(8,128)(2,1)S(1)}, bf16[512,256]{1,0:T(8,128)(2,1)S(1)}, u32[]{:S(2)}, u32[]{:S(2)}) collective-permute-start(bf16[512,256]{1,0:T(8,128)(2,1)S(1)} %add_convert_fusion), channel_id=1, source_target_pairs={{0,32},{8,40},{16,48},{24,56},{32,0},{40,8},{48,16},{56,24},{64,96... | collective-permute-start | bytes 786440 | tf_op jit(solution)/shard_map/ppermute | solution.py:40
  141.0 12.1 %collective-permute-start.28 = (bf16[384,256]{1,0:T(8,128)(2,1)S(1)}, bf16[384,256]{1,0:T(8,128)(2,1)S(1)}, u32[]{:S(2)}, u32[]{:S(2)}) collective-permute-start(bf16[384,256]{1,0:T(8,128)(2,1)S(1)} %get-tuple-element.114), channel_id=1, source_target_pairs={{0,2},{1,3},{2,4},{3,5},{4,6},{5,7},{6,0},{7,1},{8,10},{9,11},{10,... | collective-permute-start | bytes 589832 | tf_op jit(solution)/shard_map/ppermute | solution.py:36
  142.0 17.1 %collective-permute-start.29 = (bf16[384,256]{1,0:T(8,128)(2,1)S(1)}, bf16[384,256]{1,0:T(8,128)(2,1)S(1)}, u32[]{:S(2)}, u32[]{:S(2)}) collective-permute-start(bf16[384,256]{1,0:T(8,128)(2,1)S(1)} %shard_map.140.refs_4_), channel_id=1, source_target_pairs={{0,2},{1,3},{2,4},{3,5},{4,6},{5,7},{6,0},{7,1},{8,10},{9,11},{10,... | collective-permute-start | bytes 589832 | tf_op jit(solution)/shard_map/ppermute | solution.py:36
  145.1 14.5 %collective-permute-start.30 = (bf16[384,256]{1,0:T(8,128)(2,1)S(1)}, bf16[384,256]{1,0:T(8,128)(2,1)S(1)}, u32[]{:S(2)}, u32[]{:S(2)}) collective-permute-start(bf16[384,256]{1,0:T(8,128)(2,1)S(1)} %shard_map.140.refs_4_), channel_id=1, source_target_pairs={{0,4},{1,5},{2,6},{3,7},{4,0},{5,1},{6,2},{7,3},{8,12},{9,13},{10,... | collective-permute-start | bytes 589832 | tf_op jit(solution)/shard_map/ppermute | solution.py:36
  147.1 12.5 %collective-permute-start.31 = (bf16[384,256]{1,0:T(8,128)(2,1)S(1)}, bf16[384,256]{1,0:T(8,128)(2,1)S(1)}, u32[]{:S(2)}, u32[]{:S(2)}) collective-permute-start(bf16[384,256]{1,0:T(8,128)(2,1)S(1)} %shard_map.140.refs_4_), channel_id=1, source_target_pairs={{0,6},{1,7},{2,0},{3,1},{4,2},{5,3},{6,4},{7,5},{8,14},{9,15},{10,... | collective-permute-start | bytes 589832 | tf_op jit(solution)/shard_map/ppermute | solution.py:36
  153.4 13.0 %collective-permute-start.32 = (bf16[384,256]{1,0:T(8,128)(2,1)S(1)}, bf16[384,256]{1,0:T(8,128)(2,1)S(1)}, u32[]{:S(2)}, u32[]{:S(2)}) collective-permute-start(bf16[384,256]{1,0:T(8,128)(2,1)S(1)} %shard_map.141.refs_4_), channel_id=1, source_target_pairs={{0,2},{1,3},{2,4},{3,5},{4,6},{5,7},{6,0},{7,1},{8,10},{9,11},{10,... | collective-permute-start | bytes 589832 | tf_op jit(solution)/shard_map/ppermute | solution.py:36
  153.5 14.4 %collective-permute-start.33 = (bf16[384,256]{1,0:T(8,128)(2,1)S(1)}, bf16[384,256]{1,0:T(8,128)(2,1)S(1)}, u32[]{:S(2)}, u32[]{:S(2)}) collective-permute-start(bf16[384,256]{1,0:T(8,128)(2,1)S(1)} %shard_map.141.refs_4_), channel_id=1, source_target_pairs={{0,4},{1,5},{2,6},{3,7},{4,0},{5,1},{6,2},{7,3},{8,12},{9,13},{10,... | collective-permute-start | bytes 589832 | tf_op jit(solution)/shard_map/ppermute | solution.py:36
  169.6 20.5 %collective-permute-start.41 = (bf16[512,256]{1,0:T(8,128)(2,1)S(1)}, bf16[512,256]{1,0:T(8,128)(2,1)S(1)}, u32[]{:S(2)}, u32[]{:S(2)}) collective-permute-start(bf16[512,256]{1,0:T(8,128)(2,1)S(1)} %get-tuple-element.124), channel_id=1, source_target_pairs={{0,1},{1,0},{2,3},{3,2},{4,5},{5,4},{6,7},{7,6},{8,9},{9,8},{10,11... | collective-permute-start | bytes 786440 | tf_op jit(solution)/shard_map/ppermute | solution.py:29
  (21 other events, 273.9 us)
where the time goes:
time: 192 us; the launch traced here: 191 us
  waiting for transfers between devices  83.4 us (43%)
  starting transfers between devices  79.2 us (41%)
  Pallas kernels  20.8 us (11%)
  other arithmetic  3.96 us (2%)
  local copies, waits for them, and re-layouts  2.34 us (1%)
    ppermute x30, waiting for transfers between devices, x_shift(): return lax.ppermute(array, 'fsdp', pairs)  45.7 us
    ppermute x7, waiting for transfers between devices, z_swap(): return lax.ppermute(array, 'fsdp', [(i, i ^ 1) for i in range(2 * XS)])  37.7 us
    ppermute x30, starting transfers between devices, x_shift(): return lax.ppermute(array, 'fsdp', pairs)  36.4 us
    ppermute x7, starting transfers between devices, z_swap(): return lax.ppermute(array, 'fsdp', [(i, i ^ 1) for i in range(2 * XS)])  27.3 us
    ppermute x5, starting transfers between devices, rep_swap(): return lax.ppermute(array, 'rep', [(i, i ^ bit) for i in range(32)])  15.6 us
    pallas_call x4, Pallas kernels, backward(): pl.pallas_call(functools.partial(backward_body, scale), grid_spec=pltpu.P...  6.9 us
    pallas_call x4, Pallas kernels, forward(): pl.pallas_call(forward_body, grid_spec=pltpu.PrefetchScalarGridSpec(num_s...  4.98 us
  transfers between devices with their start and end apart: 42, of which 18 were waited for; matrix products, arithmetic and copies ran while one was open for 3% of the time, Pallas kernels for 8%

commit v1 on v0

--- a/solution.py
+++ b/solution.py
@@ -339,7 +339,7 @@
             grads[c] = backward(proj_scale, z_at, blocks, spread_backs)
             last = grads[c][0]
         if step + 1 < steps:
-            blocks_next = spread([after(cut, *spread_backs) for cut in cuts[step + 1]])
+            blocks_next = spread([after(cut, grads[0][1]) for cut in cuts[step + 1]])
         for c in range(CHUNKS):
             first, second, weight, other, column = state[c]
             mine, theirs = grads[c]

time: 192 us -> 191 us (level)
  the two profiles are of different devices: /device:TPU:1 before, /device:TPU:80 now
where the time goes in v1:
time: 191 us
  waiting for transfers between devices  83.7 us (44%)
  starting transfers between devices  78.8 us (41%)
  Pallas kernels  20.7 us (11%)
  other arithmetic  3.97 us (2%)
  local copies, waits for them, and re-layouts  2.34 us (1%)
    ppermute x7, waiting for transfers between devices, z_swap(): return lax.ppermute(array, 'fsdp', [(i, i ^ 1) for i in range(2 * XS)])  57.9 us
    ppermute x30, starting transfers between devices, x_shift(): return lax.ppermute(array, 'fsdp', pairs)  48.6 us
    ppermute x30, waiting for transfers between devices, x_shift(): return lax.ppermute(array, 'fsdp', pairs)  25.7 us
    ppermute x7, starting transfers between devices, z_swap(): return lax.ppermute(array, 'fsdp', [(i, i ^ 1) for i in range(2 * XS)])  25.6 us
    pallas_call x4, Pallas kernels, backward(): pl.pallas_call(functools.partial(backward_body, scale), grid_spec=pltpu.P...  6.86 us
    pallas_call x4, Pallas kernels, forward(): pl.pallas_call(forward_body, grid_spec=pltpu.PrefetchScalarGridSpec(num_s...  5 us
    ppermute x5, starting transfers between devices, rep_swap(): return lax.ppermute(array, 'rep', [(i, i ^ bit) for i in range(32)])  4.53 us
  transfers between devices with their start and end apart: 42, of which 21 were waited for; matrix products, arithmetic and copies ran while one was open for 3% of the time, Pallas kernels for 8%

profile of v1, /device:TPU:80, one launch (start us, length us, event | category | flops | bytes accessed | tf_op | source)
XLA Modules:
  0.0 191.1 jit_solution(9208619459866742795)
XLA Ops:
  0.7 3.2 %shard_map.129 = (bf16[384,1024]{1,0:T(8,128)(2,1)}, bf16[384,1024]{1,0:T(8,128)(2,1)}, bf16[384,1024]{1,0:T(8,128)(2,1)}, bf16[384,1024]{1,0:T(8,128)(2,1)}) custom-call(s32[1]{0:T(128)} %bitcast.1.x_at, bf16[1,2,384,4096]{3,2,1,0:T(8,128)(2,1)} %refs_3_.3, bf16[1,2,384,4096]{3,2,1,0:T(8,128)(2,1)} %refs_3_.3, bf16[1,2,384,4096]{3,2,1,0:T(8,128)(2,1)} %refs_3_.3, ...), custom_call_target="tpu_custom_call" | custom-call | flops 1000 | bytes 1000 | tf_op jit(solution)/shard_map/pallas_call | solution.py:68
  5.4 2.7 %collective-permute-start.1 = (bf16[384,1024]{1,0:T(8,128)(2,1)}, bf16[384,1024]{1,0:T(8,128)(2,1)S(1)}, u32[]{:S(2)}, u32[]{:S(2)}) collective-permute-start(bf16[384,1024]{1,0:T(8,128)(2,1)} %get-tuple-element.71), channel_id=1, source_target_pairs={{0,4},{1,5},{2,6},{3,7},{4,0},{5,1},{6,2},{7,3},{8,12},{9,13},{10,... | collective-permute-start | bytes 2359304 | tf_op jit(solution)/shard_map/ppermute | solution.py:36
  9.5 5.4 %collective-permute-start.3 = (bf16[512,512]{1,0:T(8,128)(2,1)S(1)}, bf16[512,512]{1,0:T(8,128)(2,1)S(1)}, u32[]{:S(2)}, u32[]{:S(2)}) collective-permute-start(bf16[512,512]{1,0:T(8,128)(2,1)S(1)} %bitcast.23), channel_id=1, source_target_pairs={{0,1},{1,0},{2,3},{3,2},{4,5},{5,4},{6,7},{7,6},{8,9},{9,8},{10,11... | collective-permute-start | bytes 1572872 | tf_op jit(solution)/shard_map/ppermute | solution.py:29
  16.3 21.3 %collective-permute-done.3.refs_5_ = bf16[512,512]{1,0:T(8,128)(2,1)S(1)} collective-permute-done((bf16[512,512]{1,0:T(8,128)(2,1)S(1)}, bf16[512,512]{1,0:T(8,128)(2,1)S(1)}, u32[]{:S(2)}, u32[]{:S(2)}) %collective-permute-start.3) | collective-permute-done | bytes 524320 | tf_op jit(solution)/shard_map/ppermute | solution.py:29
  37.7 4.8 %collective-permute-done.1.refs_2_ = bf16[384,1024]{1,0:T(8,128)(2,1)S(1)} collective-permute-done((bf16[384,1024]{1,0:T(8,128)(2,1)}, bf16[384,1024]{1,0:T(8,128)(2,1)S(1)}, u32[]{:S(2)}, u32[]{:S(2)}) %collective-permute-start.1) | collective-permute-done | bytes 786464 | tf_op jit(solution)/shard_map/ppermute | solution.py:36
  44.8 2.3 %collective-permute-start.4 = (bf16[384,256]{1,0:T(8,128)(2,1)S(1)}, bf16[384,256]{1,0:T(8,128)(2,1)S(1)}, u32[]{:S(2)}, u32[]{:S(2)}) collective-permute-start(bf16[384,256]{1,0:T(8,128)(2,1)S(1)} %get-tuple-element.77), channel_id=1, source_target_pairs={{0,6},{1,7},{2,0},{3,1},{4,2},{5,3},{6,4},{7,5},{8,14},{9,15},{10,... | collective-permute-start | bytes 589832 | tf_op jit(solution)/shard_map/ppermute | solution.py:36
  51.6 2.6 %collective-permute-start.7 = (bf16[384,256]{1,0:T(8,128)(2,1)S(1)}, bf16[384,256]{1,0:T(8,128)(2,1)S(1)}, u32[]{:S(2)}, u32[]{:S(2)}) collective-permute-start(bf16[384,256]{1,0:T(8,128)(2,1)S(1)} %get-tuple-element.81), channel_id=1, source_target_pairs={{0,6},{1,7},{2,0},{3,1},{4,2},{5,3},{6,4},{7,5},{8,14},{9,15},{10,... | collective-permute-start | bytes 589832 | tf_op jit(solution)/shard_map/ppermute | solution.py:36
  54.2 2.0 %collective-permute-done.4.refs_1_ = bf16[384,256]{1,0:T(8,128)(2,1)S(1)} collective-permute-done((bf16[384,256]{1,0:T(8,128)(2,1)S(1)}, bf16[384,256]{1,0:T(8,128)(2,1)S(1)}, u32[]{:S(2)}, u32[]{:S(2)}) %collective-permute-start.4) | collective-permute-done | bytes 196640 | tf_op jit(solution)/shard_map/ppermute | solution.py:36
  56.5 4.5 %collective-permute-start.9 = (bf16[384,256]{1,0:T(8,128)(2,1)S(1)}, bf16[384,256]{1,0:T(8,128)(2,1)S(1)}, u32[]{:S(2)}, u32[]{:S(2)}) collective-permute-start(bf16[384,256]{1,0:T(8,128)(2,1)S(1)} %get-tuple-element.83), channel_id=1, source_target_pairs={{0,2},{1,3},{2,4},{3,5},{4,6},{5,7},{6,0},{7,1},{8,10},{9,11},{10,... | collective-permute-start | bytes 589832 | tf_op jit(solution)/shard_map/ppermute | solution.py:36
  62.3 2.0 %collective-permute-start.37 = (bf16[512,256]{1,0:T(8,128)(2,1)S(1)}, bf16[512,256]{1,0:T(8,128)(2,1)S(1)}, u32[]{:S(2)}, u32[]{:S(2)}) collective-permute-start(bf16[512,256]{1,0:T(8,128)(2,1)S(1)} %add_convert_fusion.3), channel_id=1, source_target_pairs={{0,16},{8,24},{16,0},{24,8},{32,48},{40,56},{48,32},{56,40},{64,80... | collective-permute-start | bytes 786440 | tf_op jit(solution)/shard_map/ppermute | solution.py:40
  65.8 2.1 %collective-permute-start.12 = (bf16[384,256]{1,0:T(8,128)(2,1)S(1)}, bf16[384,256]{1,0:T(8,128)(2,1)S(1)}, u32[]{:S(2)}, u32[]{:S(2)}) collective-permute-start(bf16[384,256]{1,0:T(8,128)(2,1)S(1)} %shard_map.132.refs_4_), channel_id=1, source_target_pairs={{0,6},{1,7},{2,0},{3,1},{4,2},{5,3},{6,4},{7,5},{8,14},{9,15},{10,... | collective-permute-start | bytes 589832 | tf_op jit(solution)/shard_map/ppermute | solution.py:36
  69.3 4.8 %collective-permute-done.10.refs_5_ = bf16[384,256]{1,0:T(8,128)(2,1)S(1)} collective-permute-done((bf16[384,256]{1,0:T(8,128)(2,1)S(1)}, bf16[384,256]{1,0:T(8,128)(2,1)S(1)}, u32[]{:S(2)}, u32[]{:S(2)}) %collective-permute-start.10) | collective-permute-done | bytes 196640 | tf_op jit(solution)/shard_map/ppermute | solution.py:36
  74.1 1.9 collective-permute-start.17
  80.0 5.5 %collective-permute-start.19 = (bf16[512,256]{1,0:T(8,128)(2,1)S(1)}, bf16[512,256]{1,0:T(8,128)(2,1)S(1)}, u32[]{:S(2)}, u32[]{:S(2)}) collective-permute-start(bf16[512,256]{1,0:T(8,128)(2,1)S(1)} %get-tuple-element.85), channel_id=1, source_target_pairs={{0,1},{1,0},{2,3},{3,2},{4,5},{5,4},{6,7},{7,6},{8,9},{9,8},{10,11... | collective-permute-start | bytes 786440 | tf_op jit(solution)/shard_map/ppermute | solution.py:29
  86.6 2.9 %collective-permute-start.14 = (bf16[384,1024]{1,0:T(8,128)(2,1)S(1)}, bf16[384,1024]{1,0:T(8,128)(2,1)S(1)}, u32[]{:S(2)}, u32[]{:S(2)}) collective-permute-start(bf16[384,1024]{1,0:T(8,128)(2,1)S(1)} %get-tuple-element.90), channel_id=1, source_target_pairs={{0,4},{1,5},{2,6},{3,7},{4,0},{5,1},{6,2},{7,3},{8,12},{9,13},{10,... | collective-permute-start | bytes 2359304 | tf_op jit(solution)/shard_map/ppermute | solution.py:36
  94.3 5.2 %collective-permute-start.20 = (bf16[512,256]{1,0:T(8,128)(2,1)S(1)}, bf16[512,256]{1,0:T(8,128)(2,1)S(1)}, u32[]{:S(2)}, u32[]{:S(2)}) collective-permute-start(bf16[512,256]{1,0:T(8,128)(2,1)S(1)} %get-tuple-element.99), channel_id=1, source_target_pairs={{0,1},{1,0},{2,3},{3,2},{4,5},{5,4},{6,7},{7,6},{8,9},{9,8},{10,11... | collective-permute-start | bytes 786440 | tf_op jit(solution)/shard_map/ppermute | solution.py:29
  101.0 14.7 %collective-permute-done.20.received = bf16[512,256]{1,0:T(8,128)(2,1)S(1)} collective-permute-done((bf16[512,256]{1,0:T(8,128)(2,1)S(1)}, bf16[512,256]{1,0:T(8,128)(2,1)S(1)}, u32[]{:S(2)}, u32[]{:S(2)}) %collective-permute-start.20) | collective-permute-done | bytes 262176 | tf_op jit(solution)/shard_map/ppermute | solution.py:29
  117.2 5.0 %collective-permute-done.21.refs_5_ = bf16[512,256]{1,0:T(8,128)(2,1)S(1)} collective-permute-done((bf16[512,256]{1,0:T(8,128)(2,1)S(1)}, bf16[512,256]{1,0:T(8,128)(2,1)S(1)}, u32[]{:S(2)}, u32[]{:S(2)}) %collective-permute-start.21) | collective-permute-done | bytes 262176 | tf_op jit(solution)/shard_map/ppermute | solution.py:29
  122.2 3.9 %collective-permute-start.22 = (bf16[512,256]{1,0:T(8,128)(2,1)S(1)}, bf16[512,256]{1,0:T(8,128)(2,1)S(1)}, u32[]{:S(2)}, u32[]{:S(2)}) collective-permute-start(bf16[512,256]{1,0:T(8,128)(2,1)S(1)} %get-tuple-element.105.refs_4_.weight), channel_id=1, source_target_pairs={{0,1},{1,0},{2,3},{3,2},{4,5},{5,4},{6,7},{7,6},{8,9},{9,8},{10,11... | collective-permute-start | bytes 786440 | tf_op jit(solution)/shard_map/ppermute | solution.py:29
  127.4 3.1 %collective-permute-start.23 = (bf16[384,256]{1,0:T(8,128)(2,1)S(1)}, bf16[384,256]{1,0:T(8,128)(2,1)S(1)}, u32[]{:S(2)}, u32[]{:S(2)}) collective-permute-start(bf16[384,256]{1,0:T(8,128)(2,1)S(1)} %get-tuple-element.108), channel_id=1, source_target_pairs={{0,6},{1,7},{2,0},{3,1},{4,2},{5,3},{6,4},{7,5},{8,14},{9,15},{10,... | collective-permute-start | bytes 589832 | tf_op jit(solution)/shard_map/ppermute | solution.py:36
  132.0 2.8 %collective-permute-done.22.refs_5_ = bf16[512,256]{1,0:T(8,128)(2,1)S(1)} collective-permute-done((bf16[512,256]{1,0:T(8,128)(2,1)S(1)}, bf16[512,256]{1,0:T(8,128)(2,1)S(1)}, u32[]{:S(2)}, u32[]{:S(2)}) %collective-permute-start.22) | collective-permute-done | bytes 262176 | tf_op jit(solution)/shard_map/ppermute | solution.py:29
  136.0 6.5 %collective-permute-start.26 = (bf16[384,256]{1,0:T(8,128)(2,1)S(1)}, bf16[384,256]{1,0:T(8,128)(2,1)S(1)}, u32[]{:S(2)}, u32[]{:S(2)}) collective-permute-start(bf16[384,256]{1,0:T(8,128)(2,1)S(1)} %get-tuple-element.112), channel_id=1, source_target_pairs={{0,6},{1,7},{2,0},{3,1},{4,2},{5,3},{6,4},{7,5},{8,14},{9,15},{10,... | collective-permute-start | bytes 589832 | tf_op jit(solution)/shard_map/ppermute | solution.py:36
  143.9 2.5 %collective-permute-start.29 = (bf16[384,256]{1,0:T(8,128)(2,1)S(1)}, bf16[384,256]{1,0:T(8,128)(2,1)S(1)}, u32[]{:S(2)}, u32[]{:S(2)}) collective-permute-start(bf16[384,256]{1,0:T(8,128)(2,1)S(1)} %shard_map.140.refs_4_), channel_id=1, source_target_pairs={{0,2},{1,3},{2,4},{3,5},{4,6},{5,7},{6,0},{7,1},{8,10},{9,11},{10,... | collective-permute-start | bytes 589832 | tf_op jit(solution)/shard_map/ppermute | solution.py:36
  146.4 3.8 %collective-permute-done.26.refs_1_ = bf16[384,256]{1,0:T(8,128)(2,1)S(1)} collective-permute-done((bf16[384,256]{1,0:T(8,128)(2,1)S(1)}, bf16[384,256]{1,0:T(8,128)(2,1)S(1)}, u32[]{:S(2)}, u32[]{:S(2)}) %collective-permute-start.26) | collective-permute-done | bytes 196640 | tf_op jit(solution)/shard_map/ppermute | solution.py:36
  151.9 2.0 %collective-permute-start.31 = (bf16[384,256]{1,0:T(8,128)(2,1)S(1)}, bf16[384,256]{1,0:T(8,128)(2,1)S(1)}, u32[]{:S(2)}, u32[]{:S(2)}) collective-permute-start(bf16[384,256]{1,0:T(8,128)(2,1)S(1)} %shard_map.140.refs_4_), channel_id=1, source_target_pairs={{0,6},{1,7},{2,0},{3,1},{4,2},{5,3},{6,4},{7,5},{8,14},{9,15},{10,... | collective-permute-start | bytes 589832 | tf_op jit(solution)/shard_map/ppermute | solution.py:36
  155.2 3.4 %collective-permute-start.33 = (bf16[384,256]{1,0:T(8,128)(2,1)S(1)}, bf16[384,256]{1,0:T(8,128)(2,1)S(1)}, u32[]{:S(2)}, u32[]{:S(2)}) collective-permute-start(bf16[384,256]{1,0:T(8,128)(2,1)S(1)} %shard_map.141.refs_4_), channel_id=1, source_target_pairs={{0,4},{1,5},{2,6},{3,7},{4,0},{5,1},{6,2},{7,3},{8,12},{9,13},{10,... | collective-permute-start | bytes 589832 | tf_op jit(solution)/shard_map/ppermute | solution.py:36
  158.5 1.8 collective-permute-done.29.refs_5_
  161.4 3.2 %collective-permute-done.30.refs_6_ = bf16[384,256]{1,0:T(8,128)(2,1)S(1)} collective-permute-done((bf16[384,256]{1,0:T(8,128)(2,1)S(1)}, bf16[384,256]{1,0:T(8,128)(2,1)S(1)}, u32[]{:S(2)}, u32[]{:S(2)}) %collective-permute-start.30) | collective-permute-done | bytes 196640 | tf_op jit(solution)/shard_map/ppermute | solution.py:36
  166.5 3.6 %collective-permute-start.35 = (bf16[512,256]{1,0:T(8,128)(2,1)S(1)}, bf16[512,256]{1,0:T(8,128)(2,1)S(1)}, u32[]{:S(2)}, u32[]{:S(2)}) collective-permute-start(bf16[512,256]{1,0:T(8,128)(2,1)S(1)} %get-tuple-element.120), channel_id=1, source_target_pairs={{0,1},{1,0},{2,3},{3,2},{4,5},{5,4},{6,7},{7,6},{8,9},{9,8},{10,11... | collective-permute-start | bytes 786440 | tf_op jit(solution)/shard_map/ppermute | solution.py:29
  171.5 1.7 shard_map.143
  175.8 10.3 %collective-permute-done.35.received = bf16[512,256]{1,0:T(8,128)(2,1)S(1)} collective-permute-done((bf16[512,256]{1,0:T(8,128)(2,1)S(1)}, bf16[512,256]{1,0:T(8,128)(2,1)S(1)}, u32[]{:S(2)}, u32[]{:S(2)}) %collective-permute-start.35) | collective-permute-done | bytes 262176 | tf_op jit(solution)/shard_map/ppermute | solution.py:29
  187.4 2.3 %collective-permute-done.41.received = bf16[512,256]{1,0:T(8,128)(2,1)S(1)} collective-permute-done((bf16[512,256]{1,0:T(8,128)(2,1)S(1)}, bf16[512,256]{1,0:T(8,128)(2,1)S(1)}, u32[]{:S(2)}, u32[]{:S(2)}) %collective-permute-start.41) | collective-permute-done | bytes 262176 | tf_op jit(solution)/shard_map/ppermute | solution.py:29
  (105 shorter events, 45.7 us)
Async XLA Ops:
  3.9 33.8 %collective-permute-start = (bf16[384,1024]{1,0:T(8,128)(2,1)}, bf16[384,1024]{1,0:T(8,128)(2,1)S(1)}, u32[]{:S(2)}, u32[]{:S(2)}) collective-permute-start(bf16[384,1024]{1,0:T(8,128)(2,1)} %get-tuple-element.70), channel_id=1, source_target_pairs={{0,2},{1,3},{2,4},{3,5},{4,6},{5,7},{6,0},{7,1},{8,10},{9,11},{10,... | collective-permute-start | bytes 2359304 | tf_op jit(solution)/shard_map/ppermute | solution.py:36
  5.4 37.0 %collective-permute-start.1 = (bf16[384,1024]{1,0:T(8,128)(2,1)}, bf16[384,1024]{1,0:T(8,128)(2,1)S(1)}, u32[]{:S(2)}, u32[]{:S(2)}) collective-permute-start(bf16[384,1024]{1,0:T(8,128)(2,1)} %get-tuple-element.71), channel_id=1, source_target_pairs={{0,4},{1,5},{2,6},{3,7},{4,0},{5,1},{6,2},{7,3},{8,12},{9,13},{10,... | collective-permute-start | bytes 2359304 | tf_op jit(solution)/shard_map/ppermute | solution.py:36
  8.1 34.3 %collective-permute-start.2 = (bf16[384,1024]{1,0:T(8,128)(2,1)}, bf16[384,1024]{1,0:T(8,128)(2,1)S(1)}, u32[]{:S(2)}, u32[]{:S(2)}) collective-permute-start(bf16[384,1024]{1,0:T(8,128)(2,1)} %get-tuple-element.72), channel_id=1, source_target_pairs={{0,6},{1,7},{2,0},{3,1},{4,2},{5,3},{6,4},{7,5},{8,14},{9,15},{10,... | collective-permute-start | bytes 2359304 | tf_op jit(solution)/shard_map/ppermute | solution.py:36
  9.5 28.1 %collective-permute-start.3 = (bf16[512,512]{1,0:T(8,128)(2,1)S(1)}, bf16[512,512]{1,0:T(8,128)(2,1)S(1)}, u32[]{:S(2)}, u32[]{:S(2)}) collective-permute-start(bf16[512,512]{1,0:T(8,128)(2,1)S(1)} %bitcast.23), channel_id=1, source_target_pairs={{0,1},{1,0},{2,3},{3,2},{4,5},{5,4},{6,7},{7,6},{8,9},{9,8},{10,11... | collective-permute-start | bytes 1572872 | tf_op jit(solution)/shard_map/ppermute | solution.py:29
  16.3 45.0 %collective-permute-start.36 = (bf16[512,256]{1,0:T(8,128)(2,1)}, bf16[512,256]{1,0:T(8,128)(2,1)}, u32[]{:S(2)}, u32[]{:S(2)}) collective-permute-start(bf16[512,256]{1,0:T(8,128)(2,1)} %dynamic-slice_bitcast_fusion), channel_id=1, source_target_pairs={{0,8},{8,0},{16,24},{24,16},{32,40},{40,32},{48,56},{56,48},{64,72... | collective-permute-start | bytes 786440 | tf_op jit(solution)/shard_map/ppermute | solution.py:40
  48.3 12.6 %collective-permute-start.6 = (bf16[384,256]{1,0:T(8,128)(2,1)S(1)}, bf16[384,256]{1,0:T(8,128)(2,1)S(1)}, u32[]{:S(2)}, u32[]{:S(2)}) collective-permute-start(bf16[384,256]{1,0:T(8,128)(2,1)S(1)} %get-tuple-element.79), channel_id=1, source_target_pairs={{0,2},{1,3},{2,4},{3,5},{4,6},{5,7},{6,0},{7,1},{8,10},{9,11},{10,... | collective-permute-start | bytes 589832 | tf_op jit(solution)/shard_map/ppermute | solution.py:36
  51.6 12.8 %collective-permute-start.7 = (bf16[384,256]{1,0:T(8,128)(2,1)S(1)}, bf16[384,256]{1,0:T(8,128)(2,1)S(1)}, u32[]{:S(2)}, u32[]{:S(2)}) collective-permute-start(bf16[384,256]{1,0:T(8,128)(2,1)S(1)} %get-tuple-element.81), channel_id=1, source_target_pairs={{0,6},{1,7},{2,0},{3,1},{4,2},{5,3},{6,4},{7,5},{8,14},{9,15},{10,... | collective-permute-start | bytes 589832 | tf_op jit(solution)/shard_map/ppermute | solution.py:36
  61.2 12.9 %collective-permute-start.10 = (bf16[384,256]{1,0:T(8,128)(2,1)S(1)}, bf16[384,256]{1,0:T(8,128)(2,1)S(1)}, u32[]{:S(2)}, u32[]{:S(2)}) collective-permute-start(bf16[384,256]{1,0:T(8,128)(2,1)S(1)} %shard_map.132.refs_4_), channel_id=1, source_target_pairs={{0,2},{1,3},{2,4},{3,5},{4,6},{5,7},{6,0},{7,1},{8,10},{9,11},{10,... | collective-permute-start | bytes 589832 | tf_op jit(solution)/shard_map/ppermute | solution.py:36
  62.3 23.1 %collective-permute-start.37 = (bf16[512,256]{1,0:T(8,128)(2,1)S(1)}, bf16[512,256]{1,0:T(8,128)(2,1)S(1)}, u32[]{:S(2)}, u32[]{:S(2)}) collective-permute-start(bf16[512,256]{1,0:T(8,128)(2,1)S(1)} %add_convert_fusion.3), channel_id=1, source_target_pairs={{0,16},{8,24},{16,0},{24,8},{32,48},{40,56},{48,32},{56,40},{64,80... | collective-permute-start | bytes 786440 | tf_op jit(solution)/shard_map/ppermute | solution.py:40
  64.3 13.9 %collective-permute-start.11 = (bf16[384,256]{1,0:T(8,128)(2,1)S(1)}, bf16[384,256]{1,0:T(8,128)(2,1)S(1)}, u32[]{:S(2)}, u32[]{:S(2)}) collective-permute-start(bf16[384,256]{1,0:T(8,128)(2,1)S(1)} %shard_map.132.refs_4_), channel_id=1, source_target_pairs={{0,4},{1,5},{2,6},{3,7},{4,0},{5,1},{6,2},{7,3},{8,12},{9,13},{10,... | collective-permute-start | bytes 589832 | tf_op jit(solution)/shard_map/ppermute | solution.py:36
  65.8 12.5 %collective-permute-start.12 = (bf16[384,256]{1,0:T(8,128)(2,1)S(1)}, bf16[384,256]{1,0:T(8,128)(2,1)S(1)}, u32[]{:S(2)}, u32[]{:S(2)}) collective-permute-start(bf16[384,256]{1,0:T(8,128)(2,1)S(1)} %shard_map.132.refs_4_), channel_id=1, source_target_pairs={{0,6},{1,7},{2,0},{3,1},{4,2},{5,3},{6,4},{7,5},{8,14},{9,15},{10,... | collective-permute-start | bytes 589832 | tf_op jit(solution)/shard_map/ppermute | solution.py:36
  68.3 18.4 %collective-permute-start.16 = (bf16[384,256]{1,0:T(8,128)(2,1)S(1)}, bf16[384,256]{1,0:T(8,128)(2,1)S(1)}, u32[]{:S(2)}, u32[]{:S(2)}) collective-permute-start(bf16[384,256]{1,0:T(8,128)(2,1)S(1)} %shard_map.133.refs_4_), channel_id=1, source_target_pairs={{0,2},{1,3},{2,4},{3,5},{4,6},{5,7},{6,0},{7,1},{8,10},{9,11},{10,... | collective-permute-start | bytes 589832 | tf_op jit(solution)/shard_map/ppermute | solution.py:36
  74.1 15.5 %collective-permute-start.17 = (bf16[384,256]{1,0:T(8,128)(2,1)S(1)}, bf16[384,256]{1,0:T(8,128)(2,1)S(1)}, u32[]{:S(2)}, u32[]{:S(2)}) collective-permute-start(bf16[384,256]{1,0:T(8,128)(2,1)S(1)} %shard_map.133.refs_4_), channel_id=1, source_target_pairs={{0,4},{1,5},{2,6},{3,7},{4,0},{5,1},{6,2},{7,3},{8,12},{9,13},{10,... | collective-permute-start | bytes 589832 | tf_op jit(solution)/shard_map/ppermute | solution.py:36
  80.0 14.3 %collective-permute-start.19 = (bf16[512,256]{1,0:T(8,128)(2,1)S(1)}, bf16[512,256]{1,0:T(8,128)(2,1)S(1)}, u32[]{:S(2)}, u32[]{:S(2)}) collective-permute-start(bf16[512,256]{1,0:T(8,128)(2,1)S(1)} %get-tuple-element.85), channel_id=1, source_target_pairs={{0,1},{1,0},{2,3},{3,2},{4,5},{5,4},{6,7},{7,6},{8,9},{9,8},{10,11... | collective-permute-start | bytes 786440 | tf_op jit(solution)/shard_map/ppermute | solution.py:29
  85.5 40.6 %collective-permute-start.15 = (bf16[384,1024]{1,0:T(8,128)(2,1)S(1)}, bf16[384,1024]{1,0:T(8,128)(2,1)S(1)}, u32[]{:S(2)}, u32[]{:S(2)}) collective-permute-start(bf16[384,1024]{1,0:T(8,128)(2,1)S(1)} %get-tuple-element.92), channel_id=1, source_target_pairs={{0,6},{1,7},{2,0},{3,1},{4,2},{5,3},{6,4},{7,5},{8,14},{9,15},{10,... | collective-permute-start | bytes 2359304 | tf_op jit(solution)/shard_map/ppermute | solution.py:36
  86.6 39.5 %collective-permute-start.14 = (bf16[384,1024]{1,0:T(8,128)(2,1)S(1)}, bf16[384,1024]{1,0:T(8,128)(2,1)S(1)}, u32[]{:S(2)}, u32[]{:S(2)}) collective-permute-start(bf16[384,1024]{1,0:T(8,128)(2,1)S(1)} %get-tuple-element.90), channel_id=1, source_target_pairs={{0,4},{1,5},{2,6},{3,7},{4,0},{5,1},{6,2},{7,3},{8,12},{9,13},{10,... | collective-permute-start | bytes 2359304 | tf_op jit(solution)/shard_map/ppermute | solution.py:36
  89.6 36.5 %collective-permute-start.13 = (bf16[384,1024]{1,0:T(8,128)(2,1)S(1)}, bf16[384,1024]{1,0:T(8,128)(2,1)S(1)}, u32[]{:S(2)}, u32[]{:S(2)}) collective-permute-start(bf16[384,1024]{1,0:T(8,128)(2,1)S(1)} %get-tuple-element.88), channel_id=1, source_target_pairs={{0,2},{1,3},{2,4},{3,5},{4,6},{5,7},{6,0},{7,1},{8,10},{9,11},{10,... | collective-permute-start | bytes 2359304 | tf_op jit(solution)/shard_map/ppermute | solution.py:36
  94.3 21.4 %collective-permute-start.20 = (bf16[512,256]{1,0:T(8,128)(2,1)S(1)}, bf16[512,256]{1,0:T(8,128)(2,1)S(1)}, u32[]{:S(2)}, u32[]{:S(2)}) collective-permute-start(bf16[512,256]{1,0:T(8,128)(2,1)S(1)} %get-tuple-element.99), channel_id=1, source_target_pairs={{0,1},{1,0},{2,3},{3,2},{4,5},{5,4},{6,7},{7,6},{8,9},{9,8},{10,11... | collective-permute-start | bytes 786440 | tf_op jit(solution)/shard_map/ppermute | solution.py:29
  100.1 22.1 %collective-permute-start.21 = (bf16[512,256]{1,0:T(8,128)(2,1)S(1)}, bf16[512,256]{1,0:T(8,128)(2,1)S(1)}, u32[]{:S(2)}, u32[]{:S(2)}) collective-permute-start(bf16[512,256]{1,0:T(8,128)(2,1)S(1)} %get-tuple-element.103.refs_4_.weight), channel_id=1, source_target_pairs={{0,1},{1,0},{2,3},{3,2},{4,5},{5,4},{6,7},{7,6},{8,9},{9,8},{10,11... | collective-permute-start | bytes 786440 | tf_op jit(solution)/shard_map/ppermute | solution.py:29
  115.7 15.9 %collective-permute-start.39 = (bf16[512,256]{1,0:T(8,128)(2,1)S(1)}, bf16[512,256]{1,0:T(8,128)(2,1)S(1)}, u32[]{:S(2)}, u32[]{:S(2)}) collective-permute-start(bf16[512,256]{1,0:T(8,128)(2,1)S(1)} %add_convert_fusion.1), channel_id=1, source_target_pairs={{0,128},{8,136},{16,144},{24,152},{32,160},{40,168},{48,176},{56,1... | collective-permute-start | bytes 786440 | tf_op jit(solution)/shard_map/ppermute | solution.py:40
  122.2 12.6 %collective-permute-start.22 = (bf16[512,256]{1,0:T(8,128)(2,1)S(1)}, bf16[512,256]{1,0:T(8,128)(2,1)S(1)}, u32[]{:S(2)}, u32[]{:S(2)}) collective-permute-start(bf16[512,256]{1,0:T(8,128)(2,1)S(1)} %get-tuple-element.105.refs_4_.weight), channel_id=1, source_target_pairs={{0,1},{1,0},{2,3},{3,2},{4,5},{5,4},{6,7},{7,6},{8,9},{9,8},{10,11... | collective-permute-start | bytes 786440 | tf_op jit(solution)/shard_map/ppermute | solution.py:29
  127.4 15.2 %collective-permute-start.23 = (bf16[384,256]{1,0:T(8,128)(2,1)S(1)}, bf16[384,256]{1,0:T(8,128)(2,1)S(1)}, u32[]{:S(2)}, u32[]{:S(2)}) collective-permute-start(bf16[384,256]{1,0:T(8,128)(2,1)S(1)} %get-tuple-element.108), channel_id=1, source_target_pairs={{0,6},{1,7},{2,0},{3,1},{4,2},{5,3},{6,4},{7,5},{8,14},{9,15},{10,... | collective-permute-start | bytes 589832 | tf_op jit(solution)/shard_map/ppermute | solution.py:36
  130.4 12.1 %collective-permute-start.24 = (bf16[384,256]{1,0:T(8,128)(2,1)S(1)}, bf16[384,256]{1,0:T(8,128)(2,1)S(1)}, u32[]{:S(2)}, u32[]{:S(2)}) collective-permute-start(bf16[384,256]{1,0:T(8,128)(2,1)S(1)} %get-tuple-element.109), channel_id=1, source_target_pairs={{0,4},{1,5},{2,6},{3,7},{4,0},{5,1},{6,2},{7,3},{8,12},{9,13},{10,... | collective-permute-start | bytes 589832 | tf_op jit(solution)/shard_map/ppermute | solution.py:36
  131.7 23.5 %collective-permute-start.40 = (bf16[512,256]{1,0:T(8,128)(2,1)S(1)}, bf16[512,256]{1,0:T(8,128)(2,1)S(1)}, u32[]{:S(2)}, u32[]{:S(2)}) collective-permute-start(bf16[512,256]{1,0:T(8,128)(2,1)S(1)} %add_convert_fusion), channel_id=1, source_target_pairs={{0,32},{8,40},{16,48},{24,56},{32,0},{40,8},{48,16},{56,24},{64,96... | collective-permute-start | bytes 786440 | tf_op jit(solution)/shard_map/ppermute | solution.py:40
  136.0 14.2 %collective-permute-start.26 = (bf16[384,256]{1,0:T(8,128)(2,1)S(1)}, bf16[384,256]{1,0:T(8,128)(2,1)S(1)}, u32[]{:S(2)}, u32[]{:S(2)}) collective-permute-start(bf16[384,256]{1,0:T(8,128)(2,1)S(1)} %get-tuple-element.112), channel_id=1, source_target_pairs={{0,6},{1,7},{2,0},{3,1},{4,2},{5,3},{6,4},{7,5},{8,14},{9,15},{10,... | collective-permute-start | bytes 589832 | tf_op jit(solution)/shard_map/ppermute | solution.py:36
  143.9 16.4 %collective-permute-start.29 = (bf16[384,256]{1,0:T(8,128)(2,1)S(1)}, bf16[384,256]{1,0:T(8,128)(2,1)S(1)}, u32[]{:S(2)}, u32[]{:S(2)}) collective-permute-start(bf16[384,256]{1,0:T(8,128)(2,1)S(1)} %shard_map.140.refs_4_), channel_id=1, source_target_pairs={{0,2},{1,3},{2,4},{3,5},{4,6},{5,7},{6,0},{7,1},{8,10},{9,11},{10,... | collective-permute-start | bytes 589832 | tf_op jit(solution)/shard_map/ppermute | solution.py:36
  150.2 14.5 %collective-permute-start.30 = (bf16[384,256]{1,0:T(8,128)(2,1)S(1)}, bf16[384,256]{1,0:T(8,128)(2,1)S(1)}, u32[]{:S(2)}, u32[]{:S(2)}) collective-permute-start(bf16[384,256]{1,0:T(8,128)(2,1)S(1)} %shard_map.140.refs_4_), channel_id=1, source_target_pairs={{0,4},{1,5},{2,6},{3,7},{4,0},{5,1},{6,2},{7,3},{8,12},{9,13},{10,... | collective-permute-start | bytes 589832 | tf_op jit(solution)/shard_map/ppermute | solution.py:36
  151.9 12.9 %collective-permute-start.31 = (bf16[384,256]{1,0:T(8,128)(2,1)S(1)}, bf16[384,256]{1,0:T(8,128)(2,1)S(1)}, u32[]{:S(2)}, u32[]{:S(2)}) collective-permute-start(bf16[384,256]{1,0:T(8,128)(2,1)S(1)} %shard_map.140.refs_4_), channel_id=1, source_target_pairs={{0,6},{1,7},{2,0},{3,1},{4,2},{5,3},{6,4},{7,5},{8,14},{9,15},{10,... | collective-permute-start | bytes 589832 | tf_op jit(solution)/shard_map/ppermute | solution.py:36
  154.3 15.8 %collective-permute-start.32 = (bf16[384,256]{1,0:T(8,128)(2,1)S(1)}, bf16[384,256]{1,0:T(8,128)(2,1)S(1)}, u32[]{:S(2)}, u32[]{:S(2)}) collective-permute-start(bf16[384,256]{1,0:T(8,128)(2,1)S(1)} %shard_map.141.refs_4_), channel_id=1, source_target_pairs={{0,2},{1,3},{2,4},{3,5},{4,6},{5,7},{6,0},{7,1},{8,10},{9,11},{10,... | collective-permute-start | bytes 589832 | tf_op jit(solution)/shard_map/ppermute | solution.py:36
  155.2 15.6 %collective-permute-start.33 = (bf16[384,256]{1,0:T(8,128)(2,1)S(1)}, bf16[384,256]{1,0:T(8,128)(2,1)S(1)}, u32[]{:S(2)}, u32[]{:S(2)}) collective-permute-start(bf16[384,256]{1,0:T(8,128)(2,1)S(1)} %shard_map.141.refs_4_), channel_id=1, source_target_pairs={{0,4},{1,5},{2,6},{3,7},{4,0},{5,1},{6,2},{7,3},{8,12},{9,13},{10,... | collective-permute-start | bytes 589832 | tf_op jit(solution)/shard_map/ppermute | solution.py:36
  166.5 19.5 %collective-permute-start.35 = (bf16[512,256]{1,0:T(8,128)(2,1)S(1)}, bf16[512,256]{1,0:T(8,128)(2,1)S(1)}, u32[]{:S(2)}, u32[]{:S(2)}) collective-permute-start(bf16[512,256]{1,0:T(8,128)(2,1)S(1)} %get-tuple-element.120), channel_id=1, source_target_pairs={{0,1},{1,0},{2,3},{3,2},{4,5},{5,4},{6,7},{7,6},{8,9},{9,8},{10,11... | collective-permute-start | bytes 786440 | tf_op jit(solution)/shard_map/ppermute | solution.py:29
  173.2 16.5 %collective-permute-start.41 = (bf16[512,256]{1,0:T(8,128)(2,1)S(1)}, bf16[512,256]{1,0:T(8,128)(2,1)S(1)}, u32[]{:S(2)}, u32[]{:S(2)}) collective-permute-start(bf16[512,256]{1,0:T(8,128)(2,1)S(1)} %get-tuple-element.124), channel_id=1, source_target_pairs={{0,1},{1,0},{2,3},{3,2},{4,5},{5,4},{6,7},{7,6},{8,9},{9,8},{10,11... | collective-permute-start | bytes 786440 | tf_op jit(solution)/shard_map/ppermute | solution.py:29
  (21 other events, 299.5 us)
